TPU v7x, 512 devices: a whole 4x4x16 slice. The times are simulated.
512 devices in a mesh: grp: 16 (over y, x), node: 32 (over z, core).
Axes of the slice: x: 4, y: 4, z: 16, core: 2. Of those that a mesh axis runs over, the one named last changes fastest.
Arguments:
- damage: bfloat16 [4096, 65536], P('grp', 'node'), may hold values from -6 to 6
- basis_table: bfloat16 [4096, 512], P('grp'), may hold values from -6 to 6
- train_ids: int32 [4096], P('grp'), may hold values from 0 to 4095, each once
- counts: int32 [16], replicated, may hold values from 64 to 256
- new_table: bfloat16 [2048, 512], replicated, may hold values from -6 to 6
- new_ids: int32 [1024], replicated, may hold values from 0 to 2047
Outputs:
- surrogate: bfloat16 [1024, 65536], P('grp', 'node')
- peak: float32 [1024], P('grp')
- spread: float32 [1024], P('grp')
Inputs may be any that keep to these rules, and one draw needn't show every extreme that they name: `train_ids`: each row of basis_table is named by exactly one slot.
All inputs are finite; a program needn't handle non-finite values.
Results may differ from a plain program's by a relative error of at most 0.0085.
Values may be sent and summed in bfloat16 or wider, within the bound.
A program may use at most 64 MiB of HBM per device.

v0:
```python
import jax
import jax.numpy as jnp
from jax import lax
from jax.sharding import PartitionSpec as P


def cut_along(value, dim, size):
    before, after = (value.shape[:dim], value.shape[dim + 1 :])
    return jnp.moveaxis(value.reshape(*before, size, -1, *after), dim, 0)


def sent_and_summed(value, axis, dim):
    blocks = cut_along(value, dim, lax.axis_size(axis))
    arrived = lax.all_to_all(blocks, axis, split_axis=0, concat_axis=0, tiled=True)
    return arrived.astype(jnp.float32).sum(axis=0)


def from_everyone(value, axis):
    size = lax.axis_size(axis)
    return lax.all_to_all(
        jnp.broadcast_to(value[None], (size, *value.shape)), axis, 0, 0, tiled=True
    )


def in_order(blocks, dim):
    dims = list(blocks.shape[1:])
    dims[dim] *= blocks.shape[0]
    return jnp.moveaxis(blocks, 0, dim).reshape(dims)


def gather_directly(value, axis, dim):
    blocks = from_everyone(value, axis)
    return in_order(blocks, dim)


def collected_together(value, axis):
    leaves = jax.tree.leaves(value)
    sequence = sorted(range(len(leaves)), key=lambda k: -leaves[k].size)
    width = (1, *leaves[sequence[0]].shape)[-1]
    lines = [
        jnp.pad(leaves[k].reshape(-1), (0, -leaves[k].size % width)).reshape(-1, width)
        for k in sequence
    ]
    both, at, found = (from_everyone(jnp.concatenate(lines), axis), 0, {})
    for k, line in zip(sequence, lines):
        section = both[:, at : at + len(line)].reshape(len(both), -1)
        found[k] = section[:, : leaves[k].size].reshape(-1, *leaves[k].shape)
        at += len(line)
    numbers = iter(range(len(leaves)))
    return jax.tree.map(lambda _: found[next(numbers)], value)


def folded_in_pairs(pieces, combine):
    while len(jax.tree.leaves(pieces)[0]) > 1:
        pieces = jax.vmap(combine)(
            *(jax.tree.map(lambda part: part[side::2], pieces) for side in (0, 1))
        )
    return jax.tree.map(lambda part: part[0], pieces)


def joined_all(value, axis, combine):
    pieces = collected_together(value, axis)
    return folded_in_pairs(pieces, combine)


def combine_stats(first, second):
    return (first[0] + second[0], jnp.maximum(first[1], second[1]))


def local(damage, basis_table, train_ids, counts, new_table, new_ids):
    slot_count = damage.shape[0]
    node_cells = damage.shape[1]
    group_index = lax.axis_index("grp")
    group_total = lax.axis_size("grp")
    total_nodes = node_cells * lax.axis_size("node")
    per_group = new_ids.shape[0] // group_total
    sample_total = jnp.sum(counts).astype(jnp.float32)
    basis_whole, ids_whole = (
        lax.all_gather(basis_table, "grp", axis=0, tiled=True),
        lax.all_gather(train_ids, "grp", axis=0, tiled=True),
    )
    my_slot_ids = lax.dynamic_slice_in_dim(ids_whole, group_index * slot_count, slot_count, 0)
    live_slot = jnp.arange(slot_count, dtype=jnp.int32) < counts[group_index]
    chosen = jnp.take(basis_whole, my_slot_ids, axis=0)
    weighted = jnp.where(live_slot[:, None], chosen, jnp.zeros_like(chosen))
    my_ids = lax.dynamic_slice_in_dim(new_ids, group_index * per_group, per_group, 0)
    new_rows = jnp.take(new_table, my_ids, axis=0)
    term_cols = weighted
    product = lax.dot_general(
        term_cols, damage, (((0,), (0,)), ((), ())), preferred_element_type=jnp.float32
    )
    coef_share = sent_and_summed((product / sample_total).astype(jnp.bfloat16), "grp", 0)
    term_cols = new_rows
    values = jnp.dot(
        term_cols,
        gather_directly(coef_share.astype(jnp.bfloat16), "grp", 0),
        preferred_element_type=jnp.float32,
    )
    local_square = jnp.sum(values * values, axis=1)
    local_peak = jnp.max(values, axis=1)
    squares, peak_value = joined_all((local_square, local_peak), "node", combine_stats)
    surrogate = values.astype(jnp.bfloat16)
    spread = jnp.sqrt(squares / total_nodes + 1e-06)
    return (surrogate, peak_value, spread)


def solution(mesh):
    placed = (P("grp", "node"), P("grp", None), P("grp"), P(), P(), P())
    return jax.shard_map(
        local,
        mesh=mesh,
        in_specs=placed,
        out_specs=(P("grp", "node"), P("grp"), P("grp")),
        check_vma=False,
    )
```

profile of v0, /device:TPU:1, one launch (start us, length us, event | category | flops | bytes accessed | tf_op | source)
XLA Modules:
  0.0 196.4 jit_solution(9732886169708049763)
XLA Ops:
  7.2 0.0 copy-start
  7.2 0.0 copy-start.1
  7.2 0.0 all-gather.3.cloned.1.call-start
  7.2 0.7 all-gather.3.cloned.1.call-update
  7.9 1.3 reduce_sum.30
  9.2 1.2 dynamic_slice.10
  11.1 19.1 %all-gather = s32[16,1,256]{2,1,0:T(1,128)S(1)} all-gather(s32[1,1,256]{2,1,0:T(1,128)} %bitcast.23), channel_id=1, replica_groups=mesh['grp'=16,'node'=32] {'grp'}, dimensions={0}, use_global_device_ids=true | all-gather | bytes 17408 | tf_op jit(solution)/shard_map/all_gather | solution.py:80
  30.2 0.7 compare_and_fusion
  30.9 52.3 %all-gather.3.cloned.1.call-done = bf16[4096,512]{1,0:T(8,128)(2,1)} async-done(((bf16[256,512]{1,0:T(8,128)(2,1)}), bf16[4096,512]{1,0:T(8,128)(2,1)}) %all-gather.3.cloned.1.call-update) | async-done | bytes 4194320 | tf_op jit(solution)/shard_map/all_gather | solution.py:79
  83.2 3.9 %gather_fusion.1 = bf16[256,512]{1,0:T(8,128)(2,1)S(1)} fusion(bf16[4096,512]{1,0:T(8,128)(2,1)} %all-gather.3.cloned.1.call-done, s32[1024]{0:T(1024)S(1)} %pad_clamp_fusion), kind=kCustom, calls=%fused_computation.1 | custom fusion | bytes 525312 | tf_op jit(solution)/shard_map/jit(_take)/gather | solution.py:84
  87.2 0.0 copy-done.1
  87.2 0.9 divide_convert_fusion
  88.0 32.2 %all_to_all.15 = bf16[16,32,2048]{2,1,0:T(8,128)(2,1)} all-to-all(bf16[16,32,2048]{2,1,0:T(8,128)(2,1)S(1)} %bitcast.15), channel_id=1, replica_groups=mesh['grp'=16,'node'=32] {'grp'}, dimensions={0} | all-to-all | bytes 4194304 | tf_op jit(solution)/shard_map/all_to_all | solution.py:14
  120.3 2.0 %reduce_sum.31 = bf16[32,2048]{1,0:T(8,128)(2,1)S(1)} reduce(bf16[16,32,2048]{2,1,0:T(8,128)(2,1)} %all_to_all.15, bf16[]{:T(256)} %constant.53.clone.1), dimensions={0}, to_apply=%region_1.2 | reduce | flops 983040 | bytes 2228226 | tf_op jit(solution)/shard_map/reduce_sum | solution.py:15
  122.3 1.6 broadcast_in_dim.56
  123.8 4.4 %all-to-all-start.1 = ((bf16[16,32,2048]{2,1,0:T(8,128)(2,1)}), bf16[16,32,2048]{2,1,0:T(8,128)(2,1)}, u32[]{:S(2)}, u32[]{:S(2)}) async-start(bf16[16,32,2048]{2,1,0:T(8,128)(2,1)} %broadcast_in_dim.56), calls=%async_computation.1 | async-start | bytes 4194304 | tf_op jit(solution)/shard_map/all_to_all | solution.py:20
  128.2 0.8 compare_and_fusion.1
  129.0 0.0 copy-done
  129.0 0.7 gather_fusion
  129.7 25.8 %all-to-all-done.1 = bf16[16,32,2048]{2,1,0:T(8,128)(2,1)} async-done(((bf16[16,32,2048]{2,1,0:T(8,128)(2,1)}), bf16[16,32,2048]{2,1,0:T(8,128)(2,1)}, u32[]{:S(2)}, u32[]{:S(2)}) %all-to-all-start.1) | async-done | bytes 2097184 | tf_op jit(solution)/shard_map/all_to_all | solution.py:20
  155.5 2.9 %multiply_reduce_fusion = (f32[64]{0:T(128)S(1)}, f32[64]{0:T(128)S(1)}, bf16[64,2048]{1,0:T(8,128)(2,1)}) fusion(bf16[512,2048]{1,0:T(8,128)(2,1)} %bitcast.4, bf16[64,512]{1,0:T(8,128)(2,1)S(1)} %gather_fusion, pred[64]{0:T(512)(128)(4,1)S(1)} %get-tuple-element.5), kind=kOutput, calls=%fused_computation.3 | convolution fusion | flops 134774656 | bytes 2425408 | tf_op jit(solution)/shard_map/dot_general | solution.py:94
  158.5 0.1 reshape.71
  158.6 28.3 %all_to_all.16 = f32[32,1,128]{2,1,0:T(1,128)S(1)} all-to-all(f32[32,1,128]{2,1,0:T(1,128)S(1)} %reshape.71), channel_id=1, replica_groups=mesh['grp'=16,'node'=32] {'node'}, dimensions={0} | all-to-all | bytes 32768 | tf_op jit(solution)/shard_map/all_to_all | solution.py:20
  186.8 0.5 broadcast.26
  187.3 0.7 reduce.1
  188.0 0.1 reshape.72
  188.5 0.5 sqrt_bitcast_fusion
  189.0 0.5 maximum_bitcast_fusion
  (29 shorter events, 0.4 us)
Async XLA Ops:
  7.2 121.9 %copy-start = (bf16[2048,512]{1,0:T(8,128)(2,1)S(1)}, bf16[2048,512]{1,0:T(8,128)(2,1)}, u32[]{:S(2)}) copy-start(bf16[2048,512]{1,0:T(8,128)(2,1)} %param.10) | copy-start | bytes 6291460
  7.2 80.0 %copy-start.1 = (bf16[256,2048]{1,0:T(8,128)(2,1)S(1)}, bf16[256,2048]{1,0:T(8,128)(2,1)}, u32[]{:S(2)}) copy-start(bf16[256,2048]{1,0:T(8,128)(2,1)} %param.6) | copy-start | bytes 3145732
  7.2 76.0 %all-gather.3.cloned.1.call-start = ((), (), s32[]{:S(2)}) async-start(), calls=%async_computation.3 | async-start | bytes 4456448 | tf_op jit(solution)/shard_map/all_gather | solution.py:79
  123.8 31.7 %all-to-all-start.1 = ((bf16[16,32,2048]{2,1,0:T(8,128)(2,1)}), bf16[16,32,2048]{2,1,0:T(8,128)(2,1)}, u32[]{:S(2)}, u32[]{:S(2)}) async-start(bf16[16,32,2048]{2,1,0:T(8,128)(2,1)} %broadcast_in_dim.56), calls=%async_computation.1 | async-start | bytes 4194304 | tf_op jit(solution)/shard_map/all_to_all | solution.py:20
Sparse Core Ops, SparseCore 0:
  11.0 72.1 all-gather.2
where the time goes:
time: 197 us; the launch traced here: 196 us
  blocking collectives  79.6 us (40%)
  waiting for transfers between devices  78.7 us (40%)
  between operations  14.8 us (8%)
  local copies, waits for them, and re-layouts  8.48 us (4%)
  other arithmetic  6.56 us (3%)
  starting transfers between devices  4.46 us (2%)
  matrix products  3.8 us (2%)
    all_gather x1, waiting for transfers between devices, local(): lax.all_gather(basis_table, 'grp', axis=0, tiled=True)  52.3 us
    all_to_all x1, blocking collectives, sent_and_summed(): lax.all_to_all(blocks, axis, split_axis=0, concat_axis=0, tiled=True)  32.2 us
    all_to_all x1, blocking collectives, from_everyone(): lax.all_to_all(jnp.broadcast_to(value[None], (size, *value.shape)), axis,...  28.3 us
    all_to_all x1, waiting for transfers between devices, from_everyone(): lax.all_to_all(jnp.broadcast_to(value[None], (size, *value.shape)), axis,...  25.8 us
    all_gather x1, blocking collectives, local(): lax.all_gather(train_ids, 'grp', axis=0, tiled=True)  19.1 us
    all_to_all x1, starting transfers between devices, from_everyone(): lax.all_to_all(jnp.broadcast_to(value[None], (size, *value.shape)), axis,...  4.42 us
  transfers between devices with their start and end apart: 2, of which 2 were waited for; matrix products, arithmetic and copies ran while one was open for 2% of the time, Pallas kernels for 0%

commit v1 on v0

--- a/solution.py
+++ b/solution.py
@@ -1,7 +1,19 @@
+import functools
 import jax
 import jax.numpy as jnp
 from jax import lax
 from jax.sharding import PartitionSpec as P
+
+
+def _direct_samples_all(my_tile, dim_k):
+    tile_out = jnp.stack([my_tile] * lax.psum(1, axis_name="grp"), axis=0)
+    finding = jnp.concatenate(
+        lax.all_to_all(tile_out, axis_name="grp", split_axis=0, concat_axis=0), axis=dim_k
+    )
+    return finding
+
+
+measure_the_members_all = functools.partial(_direct_samples_all, dim_k=0)
 
 
 def cut_along(value, dim, size):
@@ -76,7 +88,7 @@
     per_group = new_ids.shape[0] // group_total
     sample_total = jnp.sum(counts).astype(jnp.float32)
     basis_whole, ids_whole = (
-        lax.all_gather(basis_table, "grp", axis=0, tiled=True),
+        measure_the_members_all(basis_table),
         lax.all_gather(train_ids, "grp", axis=0, tiled=True),
     )
     my_slot_ids = lax.dynamic_slice_in_dim(ids_whole, group_index * slot_count, slot_count, 0)

time: 197 us -> 188 us (0.954)
  waiting for transfers between devices: 78.7 us -> 21.6 us
  blocking collectives: 79.6 us -> 132 us
  between operations: 14.8 us -> 1.44 us
  starting transfers between devices: 4.46 us -> 12.2 us
  local copies, waits for them, and re-layouts: 8.48 us -> 11.3 us
    all_gather x1 -> x0, waiting for transfers between devices: 52.3 us -> none  [local(): lax.all_gather(basis_table, 'grp', axis=0, tiled=True)]
    all_gather x1, blocking collectives: 19.1 us -> 63.8 us  [local(): lax.all_gather(train_ids, 'grp', axis=0, tiled=True)]
    all_to_all x1, blocking collectives: 28.3 us -> 42.2 us  [from_everyone(): lax.all_to_all(jnp.broadcast_to(value[None], (size, *value.shape)), axis,...]
    all_to_all x0 -> x1, starting transfers between devices: none -> 7.77 us  [_direct_samples_all(): lax.all_to_all(tile_out, axis_name='grp', split_axis=0, concat_axis=0)]
    all_to_all x1, blocking collectives: 32.2 us -> 25.6 us  [sent_and_summed(): lax.all_to_all(blocks, axis, split_axis=0, concat_axis=0, tiled=True)]
    all_to_all x1, waiting for transfers between devices: 25.8 us -> 21.6 us  [from_everyone(): lax.all_to_all(jnp.broadcast_to(value[None], (size, *value.shape)), axis,...]
    another operation x0 -> x1, local copies, waits for them, and re-layouts: none -> 3.47 us  [_direct_samples_all(): tile_out = jnp.stack([my_tile] * lax.psum(1, axis_name='grp'), axis=0)]
  transfers between devices with their start and end apart: 2 -> 2, of which waited for: 2 -> 1; matrix products, arithmetic and copies ran while one was open for 2% -> 2% of each run, Pallas kernels for 0% -> 0%
where the time goes in v1:
time: 188 us
  blocking collectives  132 us (70%)
  waiting for transfers between devices  21.6 us (11%)
  starting transfers between devices  12.2 us (6%)
  local copies, waits for them, and re-layouts  11.3 us (6%)
  other arithmetic  5.9 us (3%)
  matrix products  3.8 us (2%)
    all_gather x1, blocking collectives, local(): lax.all_gather(train_ids, 'grp', axis=0, tiled=True)  63.8 us
    all_to_all x1, blocking collectives, from_everyone(): lax.all_to_all(jnp.broadcast_to(value[None], (size, *value.shape)), axis,...  42.2 us
    all_to_all x1, blocking collectives, sent_and_summed(): lax.all_to_all(blocks, axis, split_axis=0, concat_axis=0, tiled=True)  25.6 us
    all_to_all x1, waiting for transfers between devices, from_everyone(): lax.all_to_all(jnp.broadcast_to(value[None], (size, *value.shape)), axis,...  21.6 us
    all_to_all x1, starting transfers between devices, _direct_samples_all(): lax.all_to_all(tile_out, axis_name='grp', split_axis=0, concat_axis=0)  7.77 us
    all_to_all x1, starting transfers between devices, from_everyone(): lax.all_to_all(jnp.broadcast_to(value[None], (size, *value.shape)), axis,...  4.42 us
    gather x1, local copies, waits for them, and re-layouts, local(): chosen = jnp.take(basis_whole, my_slot_ids, axis=0)  3.94 us
  transfers between devices with their start and end apart: 2, of which 1 were waited for; matrix products, arithmetic and copies ran while one was open for 2% of the time, Pallas kernels for 0%

profile of v1, /device:TPU:1, one launch (start us, length us, event | category | flops | bytes accessed | tf_op | source)
XLA Modules:
  0.0 187.9 jit_solution(4517727958809750916)
XLA Ops:
  0.6 0.0 copy-start
  0.6 3.5 %stack.2 = bf16[16,256,512]{2,1,0:T(8,128)(2,1)} broadcast(bf16[256,512]{1,0:T(8,128)(2,1)} %param.7), dimensions={1,2} | broadcast | bytes 4456448 | tf_op jit(solution)/shard_map/stack | solution.py:9
  4.1 0.0 copy-start.3
  4.1 0.0 copy-start.1
  4.1 7.8 %all-to-all-start = ((bf16[16,256,512]{2,1,0:T(8,128)(2,1)}), bf16[16,256,512]{2,1,0:T(8,128)(2,1)}, u32[]{:S(2)}, u32[]{:S(2)}) async-start(bf16[16,256,512]{2,1,0:T(8,128)(2,1)} %stack.2), calls=%async_computation | async-start | bytes 8388608 | tf_op jit(solution)/shard_map/all_to_all | solution.py:11
  11.9 0.0 copy-start.2
  11.9 0.0 copy-done.3
  11.9 0.6 reduce_sum.30
  13.2 0.6 dynamic_slice.10
  13.8 0.0 copy-done.1
  13.8 63.8 %all-gather = s32[16,1,256]{2,1,0:T(1,128)S(1)} all-gather(s32[1,1,256]{2,1,0:T(1,128)S(1)} %bitcast.24), channel_id=1, replica_groups=mesh['grp'=16,'node'=32] {'grp'}, dimensions={0}, use_global_device_ids=true | all-gather | bytes 17408 | tf_op jit(solution)/shard_map/all_gather | solution.py:92
  77.7 0.7 compare_and_fusion
  78.4 0.0 all-to-all-done
  78.4 3.9 %gather_fusion.1 = bf16[256,512]{1,0:T(8,128)(2,1)S(1)} fusion(bf16[4096,512]{1,0:T(8,128)(2,1)} %bitcast.3, s32[1024]{0:T(1024)S(1)} %pad_clamp_fusion), kind=kCustom, calls=%fused_computation.1 | custom fusion | bytes 525312 | tf_op jit(solution)/shard_map/jit(_take)/gather | solution.py:96
  82.3 0.0 copy-done.2
  82.3 0.9 divide_convert_fusion
  83.2 25.6 %all_to_all.20 = bf16[16,32,2048]{2,1,0:T(8,128)(2,1)} all-to-all(bf16[16,32,2048]{2,1,0:T(8,128)(2,1)S(1)} %bitcast.16), channel_id=1, replica_groups=mesh['grp'=16,'node'=32] {'grp'}, dimensions={0} | all-to-all | bytes 4194304 | tf_op jit(solution)/shard_map/all_to_all | solution.py:26
  108.9 2.0 %reduce_sum.31 = bf16[32,2048]{1,0:T(8,128)(2,1)S(1)} reduce(bf16[16,32,2048]{2,1,0:T(8,128)(2,1)} %all_to_all.20, bf16[]{:T(256)} %constant.53.clone.1), dimensions={0}, to_apply=%region_1.2 | reduce | flops 983040 | bytes 2228226 | tf_op jit(solution)/shard_map/reduce_sum | solution.py:27
  110.9 1.6 broadcast_in_dim.56
  112.4 4.4 %all-to-all-start.2 = ((bf16[16,32,2048]{2,1,0:T(8,128)(2,1)}), bf16[16,32,2048]{2,1,0:T(8,128)(2,1)}, u32[]{:S(2)}, u32[]{:S(2)}) async-start(bf16[16,32,2048]{2,1,0:T(8,128)(2,1)} %broadcast_in_dim.56), calls=%async_computation.2 | async-start | bytes 4194304 | tf_op jit(solution)/shard_map/all_to_all | solution.py:32
  116.8 0.8 compare_and_fusion.1
  117.6 0.0 copy-done
  117.6 0.7 gather_fusion
  118.3 21.6 %all-to-all-done.2 = bf16[16,32,2048]{2,1,0:T(8,128)(2,1)} async-done(((bf16[16,32,2048]{2,1,0:T(8,128)(2,1)}), bf16[16,32,2048]{2,1,0:T(8,128)(2,1)}, u32[]{:S(2)}, u32[]{:S(2)}) %all-to-all-start.2) | async-done | bytes 2097184 | tf_op jit(solution)/shard_map/all_to_all | solution.py:32
  139.9 2.9 %multiply_reduce_fusion = (f32[64]{0:T(128)S(1)}, f32[64]{0:T(128)S(1)}, bf16[64,2048]{1,0:T(8,128)(2,1)}) fusion(bf16[512,2048]{1,0:T(8,128)(2,1)} %bitcast.5, bf16[64,512]{1,0:T(8,128)(2,1)S(1)} %gather_fusion, pred[64]{0:T(512)(128)(4,1)S(1)} %get-tuple-element.5), kind=kOutput, calls=%fused_computation.3 | convolution fusion | flops 134774656 | bytes 2425408 | tf_op jit(solution)/shard_map/dot_general | solution.py:106
  142.9 0.1 reshape.77
  143.0 42.2 %all_to_all.21 = f32[32,1,128]{2,1,0:T(1,128)S(1)} all-to-all(f32[32,1,128]{2,1,0:T(1,128)S(1)} %reshape.77), channel_id=1, replica_groups=mesh['grp'=16,'node'=32] {'node'}, dimensions={0} | all-to-all | bytes 32768 | tf_op jit(solution)/shard_map/all_to_all | solution.py:32
  185.2 0.5 broadcast.28
  185.7 0.7 reduce.1
  186.4 0.1 reshape.78
  186.9 0.5 maximum_bitcast_fusion
  187.4 0.5 sqrt_bitcast_fusion
  (29 shorter events, 0.4 us)
Async XLA Ops:
  0.6 117.0 %copy-start = (bf16[2048,512]{1,0:T(8,128)(2,1)S(1)}, bf16[2048,512]{1,0:T(8,128)(2,1)}, u32[]{:S(2)}) copy-start(bf16[2048,512]{1,0:T(8,128)(2,1)} %param.10) | copy-start | bytes 6291460
  4.1 7.8 %copy-start.3 = (s32[16]{0:T(128)S(1)}, s32[16]{0:T(128)}, u32[]{:S(2)}) copy-start(s32[16]{0:T(128)} %param.9) | copy-start | bytes 196
  4.1 9.7 %copy-start.1 = (s32[256]{0:T(256)S(1)}, s32[256]{0:T(256)}, u32[]{:S(2)}) copy-start(s32[256]{0:T(256)} %param.8) | copy-start | bytes 3076
  4.1 74.3 %all-to-all-start = ((bf16[16,256,512]{2,1,0:T(8,128)(2,1)}), bf16[16,256,512]{2,1,0:T(8,128)(2,1)}, u32[]{:S(2)}, u32[]{:S(2)}) async-start(bf16[16,256,512]{2,1,0:T(8,128)(2,1)} %stack.2), calls=%async_computation | async-start | bytes 8388608 | tf_op jit(solution)/shard_map/all_to_all | solution.py:11
  11.9 70.4 %copy-start.2 = (bf16[256,2048]{1,0:T(8,128)(2,1)S(1)}, bf16[256,2048]{1,0:T(8,128)(2,1)}, u32[]{:S(2)}) copy-start(bf16[256,2048]{1,0:T(8,128)(2,1)} %param.6) | copy-start | bytes 3145732
  112.4 27.5 %all-to-all-start.2 = ((bf16[16,32,2048]{2,1,0:T(8,128)(2,1)}), bf16[16,32,2048]{2,1,0:T(8,128)(2,1)}, u32[]{:S(2)}, u32[]{:S(2)}) async-start(bf16[16,32,2048]{2,1,0:T(8,128)(2,1)} %broadcast_in_dim.56), calls=%async_computation.2 | async-start | bytes 4194304 | tf_op jit(solution)/shard_map/all_to_all | solution.py:32
